TPU v7x, 128 devices: a whole 4x4x4 slice. The times are simulated.
128 devices in a mesh: dm: 2 (over core), bin: 64 (over x, y, z).
Axes of the slice: x: 4, y: 4, z: 4, core: 2. Of those that a mesh axis runs over, the one named last changes fastest.
Arguments:
- series: float32 [16777216], P(('dm', 'bin')), parts along dimension 0, may hold values from -6 to 6
- tap_coef: float32 [2, 16, 128], replicated, may hold values from -0.5 to 0.5
- tap_offset: int32 [16, 128], replicated, may hold values from 0 to 127, each once within a row
- harm_index: int32 [8, 524288], P(None, 'bin'), may hold values from 0 to 7, as said below
Outputs:
- summed: float32 [16, 1048576], P(None, ('dm', 'bin')), parts along dimension 1
There are 2 independent parts, one for each index of `dm`. A program takes and returns all parts, laid end to end along the dimension named above; an argument that names none is the same for every part. Nothing has to cross between parts.
Inputs may be any that keep to these rules, and one draw needn't show every extreme that they name: `harm_index`: entry (h, f) is at most h. `tap_offset`: each row holds every number below 128 once.
All inputs are finite; a program needn't handle non-finite values.
Results may differ from a plain program's by a relative error of at most 0.0014.
Values may be sent and summed in bfloat16 or wider, within the bound.
A program may use at most 256 MiB of HBM per device.

v0:
```python
import functools
import math

import jax
import jax.numpy as jnp
import numpy as np
from jax import lax
from jax.experimental import pallas as pl
from jax.experimental.pallas import tpu as pltpu
from jax.sharding import PartitionSpec as P

D = 64
TMPL = 16
TAPS = 128
HARM = 8
LENGTH = 8388608
LOCAL = LENGTH // D
ALPHA = 512
BETA = 256
ORDER = (4, 8, 7, 1, 6, 2, 5, 3)
BLOCKS = tuple((h, r) for h in ORDER for r in range(h))
NB = len(BLOCKS)
FIRST = {h: BLOCKS.index((h, 0)) for h in ORDER}
ROWS = 40
CHUNKS = ((0, 8, 0, 4), (8, 8, 4, 12), (16, 8, 12, 20), (24, 16, 20, 36))
FULL = 32767.0
FAR = (2, 1, 3, 0)
SAMPLE_BOUND = 6.0
PART_BOUND = SAMPLE_BOUND * D / math.sqrt(LENGTH)
F32 = jnp.float32
BF16 = jnp.bfloat16
F8 = jnp.float8_e4m3fn
LOW = 512.0


def np_split(x):
    x = np.asarray(x, np.float32)
    hi = x.astype(jnp.bfloat16)
    lo = (x - hi.astype(np.float32)).astype(jnp.bfloat16)
    return hi, lo


@functools.lru_cache(None)
def fft_tables():
    k1 = np.arange(D)[:, None]
    m = np.arange(LOCAL // D)[None, :]
    ang = -2 * np.pi * (k1 * m) / LENGTH
    tw1 = np.stack([np.cos(ang), np.sin(ang)]).astype(np.float32)
    k = np.arange(ALPHA)[:, None] * np.arange(ALPHA)[None, :] % ALPHA
    ang = -2 * np.pi * k / ALPHA
    c, s = np.cos(ang), np.sin(ang)
    wa = np.block([[c, -s], [s, c]])
    ang = -2 * np.pi * (np.arange(ALPHA)[:, None] * np.arange(BETA)[None, :]) / LOCAL
    tw2 = np.stack([np.cos(ang), np.sin(ang)]).astype(np.float32)
    half = BETA // 2
    ang = -2 * np.pi * (np.arange(BETA)[:, None] * np.arange(half)[None, :] % BETA) / BETA
    c, s = np.cos(ang), np.sin(ang)
    vb = np.block([[c, s], [-s, c]])
    k = k1 * (D * np.arange(D)[None, None, :] + np.arange(D)[:, None, None]) % (D * D)
    ang = -2 * np.pi * k / (D * D)
    w1 = np.stack([np.cos(ang), np.sin(ang)], axis=1) / math.sqrt(LENGTH)
    w1 = w1.reshape(D, 2, 4, 16, D)
    w1 = np.stack([w1[e][:, [(e // 16 + f) % 4 for f in FAR]] for e in range(D)]).reshape(D, 2 * D, D)
    wa = wa.reshape(2 * ALPHA, 2, 4, 128).transpose(2, 0, 1, 3).reshape(4, 2 * ALPHA, 256)
    return w1.astype(np.float32), tw1, *np_split(wa), tw2, *np_split(vb)


@functools.lru_cache(None)
def perm_tables():
    out = []
    for h in range(1, HARM + 1):
        m = np.zeros((128 * h, 128 * h), np.float32)
        a = np.arange(128)
        for r in range(h):
            m[h * a + r, 128 * r + 64 * (a % 2) + a // 2] = 1
        out.append(m.astype(jnp.bfloat16))
    return tuple(out)


@functools.lru_cache(None)
def select_tables():
    i = np.arange(64)
    e = np.zeros((NB, 128, 128), np.float32)
    ex = np.zeros((NB, 128, 128), np.float32)
    jp = np.zeros((NB, 1, 128), np.float32)
    for n, (h, r) in enumerate(BLOCKS):
        b, j = np.divmod(64 * r + i, h)
        for t in range(2):
            e[n, 64 * t + i, 64 * t + b] = 1
            ex[n, b, 64 * t + i] = 1
            jp[n, 0, 64 * t + i] = j
    return e.astype(jnp.bfloat16), ex.astype(jnp.bfloat16), jp.reshape(NB, 128)


def split(x):
    hi = x.astype(BF16)
    return hi, (x - hi.astype(F32)).astype(BF16)


def dot(a, b):
    return jnp.dot(a, b, preferred_element_type=F32)


def dot3(ah, al, bh, bl):
    return dot(ah, bh) + dot(ah, bl) + dot(al, bh)


def encode(x, bound):
    size = jnp.sqrt(jnp.sqrt(jnp.abs(x) * (1.0 / bound)))
    code = jnp.minimum(size * FULL + 0.5, FULL).astype(jnp.int32)
    return jnp.where(x < 0, -code, code)


def decode(code, bound):
    x = code.astype(F32)
    return x * jnp.abs(x) * (x * x * (bound / FULL**4))


def join(high, low):
    return (high << 16) | (low & 0xFFFF)


def parted(word):
    return word >> 16, (word << 16) >> 16


def for_partners(me, act):
    far = FAR
    x = [(me // 16 + k) % 4 * 16 for k in far]
    y = [(me // 4 + k) % 4 * 4 for k in far]
    z = [(me + k) % 4 for k in far]
    plane = [b + c for b in y for c in z][:-1]

    def row(i, carry):
        first = (me // 16 + 2 + i) % 4 * 16
        for v in plane:
            act(first + v)
        return carry

    lax.fori_loop(0, 4, row, 0)
    for v in x[:-1]:
        act(v + y[-1] + z[-1])


def exchange(me, dm, src, dst, first, rows, pitch, sems):
    target = dst.at[pl.ds(pl.multiple_of(me * pitch + first, 8), rows)]

    def start(to):
        pltpu.make_async_remote_copy(
            src_ref=src.at[pl.ds(pl.multiple_of(to * pitch + first, 8), rows)],
            dst_ref=target,
            send_sem=sems[0],
            recv_sem=sems[1],
            device_id=(dm, to),
            device_id_type=pl.DeviceIdType.MESH,
        ).start()

    for_partners(me, start)
    own = pl.ds(pl.multiple_of(me * pitch + first, 8), rows)
    dst[own, :] = src[own, :]


def wait_for(ref, rows, sem):
    part = ref.at[pl.ds(0, (D - 1) * rows)]
    pltpu.make_async_copy(part, part, sem).wait()


def make_taps(vx, taps, taps8):
    lane = lax.broadcasted_iota(jnp.int32, (64, 128), 1)

    def pair(tp, carry):
        for x in range(3):
            both = []
            for z in range(2):
                rolled = []
                for t in range(2):
                    row = vx[2 * tp + t, 3 * z + x : 3 * z + x + 1, :]
                    rolled.append(
                        pltpu.roll(jnp.broadcast_to(row, (64, 128)), 64 * t, 1, stride=1, stride_axis=0)
                    )
                v = jnp.where(lane < 64, rolled[0], rolled[1])
                high = v.astype(BF16).astype(F32)
                both.append((high, (v - high) * LOW))

            def put(ref, row, kind, tr, ti):
                ref[tp, row : row + 64, 0:128] = tr.astype(kind)
                ref[tp, row : row + 64, 128:256] = ti.astype(kind)
                ref[tp, row + 64 : row + 128, 0:128] = (-ti).astype(kind)
                ref[tp, row + 64 : row + 128, 128:256] = tr.astype(kind)

            (rh, rl), (ih, il) = both
            put(taps, 128 * x, BF16, rh * LOW, ih * LOW)
            put(taps8, 128 * x, F8, rl, il)
            put(taps8, 384 + 128 * x, F8, rh, ih)
        return carry

    lax.fori_loop(0, TMPL // 2, pair, 0)


def level_of(x):
    return jnp.ceil(jnp.log2(jnp.maximum(jnp.max(jnp.abs(x), keepdims=True), 1e-30)))


def make_tap_rows(coef, offset, vx, levels):
    lane = lax.broadcasted_iota(jnp.int32, (128, 384), 1)
    m = lane % 128
    lag = lane // 128 * 64 - jnp.where(m < 64, m, m - 128)
    lag = jnp.where(m == 64, -1, lag).astype(F32)
    where = jnp.concatenate([offset[...].astype(F32), jnp.zeros((112, 128), F32)], axis=0).T
    level = level_of(coef[...])
    factor = jnp.exp2(8.0 - level)
    levels[0:8, :] = jnp.broadcast_to(level, (8, 128))
    first = coef[...].astype(BF16)
    rest = coef[...] - first.astype(F32)
    second = rest.astype(BF16)
    third = (rest - second.astype(F32)).astype(BF16)
    lhs = jnp.concatenate([first, second, third], axis=0)
    for t in range(TMPL):
        onehot = jnp.where(where[:, t : t + 1] == lag, 1.0, 0.0).astype(BF16)
        rows = dot(lhs, onehot)
        rows = (rows[0:32] + rows[32:64] + rows[64:96]) * factor
        for z in range(2):
            for x in range(3):
                vx[t, 3 * z + x : 3 * z + x + 1, :] = rows[16 * z + t : 16 * z + t + 1, 128 * x : 128 * x + 128]


def code_samples(series, out):
    v = series[...].reshape(D, 16, 128)
    word = join(encode(v[:, :8], SAMPLE_BOUND), encode(v[:, 8:], SAMPLE_BOUND))
    out[...] = word.reshape(512, 128)


def columns(xs, w1, tw, out, me, send):
    pairs = [parted(xs[pl.ds(m, D, stride=8), :]) for m in range(8)]
    x = jnp.concatenate([p[0] for p in pairs] + [p[1] for p in pairs], axis=1)
    y = dot3(*split(w1[...]), *split(decode(x, SAMPLE_BOUND)))
    for j, far in enumerate(FAR):
        plane = (me // 16 + far) % 4
        rows = pl.ds(pl.multiple_of(16 * plane, 16), 16)
        yr, yi = y[16 * j : 16 * j + 16], y[D + 16 * j : D + 16 * j + 16]
        tr, ti = tw[0, rows, :], tw[1, rows, :]
        word = join(encode(yr * tr - yi * ti, PART_BOUND), encode(yr * ti + yi * tr, PART_BOUND))
        for m in range(16):
            out[pl.ds(256 * j + (m % 2) * 8 + m // 2, 16, stride=16), :] = word[:, 128 * m : 128 * m + 128]
        send(j, plane)


def local_fft(me, arrived, b, wah, wal, tw, vbh, vbl, yacc, zn, levels):
    for j, far in enumerate(FAR):
        arrived(j)
        plane = (me // 16 + 4 - far) % 4
        v = b[pl.ds(pl.multiple_of(256 * plane, 256), 256), :].reshape(16, 2, 8, 128)
        word = jnp.concatenate([v[:, n].reshape(128, 128) for n in range(2)], axis=1)
        rhs = jnp.concatenate([decode(x, PART_BOUND) for x in parted(word)], axis=0)
        y = dot3(wah[plane], wal[plane], *split(rhs))
        if j > 0:
            y = y + yacc[...]
        if j < 3:
            yacc[...] = y
    yr, yi = y[:ALPHA], y[ALPHA:]
    t = jnp.concatenate([yr * tw[0] - yi * tw[1], yr * tw[1] + yi * tw[0]], axis=1)
    th, tl = split(t)
    z = dot3(th, tl, vbh[...], vbl[...])
    level = level_of(z)
    levels[16:24, :] = jnp.broadcast_to(level, (8, 128))
    z = jnp.clip(jnp.round(z * (jnp.exp2(-level) * FULL)), -FULL, FULL)
    zero = jnp.zeros((8, 128), F32)
    for c in range(2):
        zt = z[:, 128 * c : 128 * c + 128].T
        zn[c, 0:8, :] = zero
        zn[c, 520:528, :] = zero
        for n in range(4):
            zn[c, pl.ds(8 + n, 128, stride=4), :] = zt[:, 128 * n : 128 * n + 128]


def pack_ends(zn, levels, out):
    lane = lax.broadcasted_iota(jnp.int32, (D, 128), 1)
    ends = jnp.broadcast_to(levels[16:17, :], (D, 128)).astype(jnp.int32)
    for h in range(1, HARM + 1):
        left = [zn[c, pl.ds(7, D, stride=h), :].astype(jnp.int32) for c in range(2)]
        right = [zn[c, pl.ds(8 + h, D, stride=h), :].astype(jnp.int32) for c in range(2)]
        ends = jnp.where(lane == h - 1, join(*left)[:, 127:128], ends)
        ends = jnp.where(lane == 8 + h - 1, join(*right)[:, 0:1], ends)
    out[pl.ds(0, D, stride=ROWS), :] = ends
    for n in range(1, 4):
        out[pl.ds(n, D, stride=ROWS), :] = jnp.zeros((D, 128), jnp.int32)


def pack_harmonic(h, zn, perm, out):
    src = jnp.concatenate(
        [
            jnp.concatenate([zn[c, pl.ds(8 + n, D, stride=h), :] for n in range(h)], axis=1)
            for c in range(2)
        ],
        axis=0,
    )
    hi, lo = split(src)
    moved = dot(jnp.concatenate([hi, lo], axis=0), perm[...])
    moved = (moved[:128] + moved[128:]).astype(jnp.int32)
    word = join(moved[:64], moved[64:])
    for r in range(h):
        out[pl.ds(4 + FIRST[h] + r, D, stride=ROWS), :] = word[:, 128 * r : 128 * r + 128]


def unpack_ends(land, ends, levels):
    lane = lax.broadcasted_iota(jnp.int32, (8, 128), 1)
    word = land[pl.ds(0, D, stride=ROWS), :]
    re, im = parted(word)
    zero = jnp.zeros((D, 128), F32)
    re, im, word = [jnp.concatenate([v.astype(F32), zero], axis=0).T for v in (re, im, word)]
    level = jnp.where(lane < 64, word[16:24], -1000.0)
    top = jnp.max(level[0:1], axis=1, keepdims=True)
    levels[8:16, :] = jnp.broadcast_to(top, (8, 128))
    scale = jnp.exp2(level - top + 8.0) * (1.0 / FULL)
    scale = jnp.where(lane < 64, scale, pltpu.roll(scale, 64, 1))
    scale = jnp.broadcast_to(scale[0:1], (8, 128))
    for n in range(2):
        part = slice(8 * n, 8 * n + 8)
        ends[part, :] = jnp.where(lane < 64, re[part], pltpu.roll(im[part], 64, 1)) * scale
    ends[16:24, :] = scale


def unpack(land, ends, first, last, side, xl, xl8):
    def put(n, slot, x):
        high = x.astype(BF16)
        wide = high.astype(F32)
        parts = (high, wide.astype(F8), ((x - wide) * LOW).astype(F8))
        return put_parts(n, slot, parts)

    def put_parts(n, slot, parts):
        xl[pl.ds(128 * n, 128), pl.ds(128 * slot, 128)] = parts[0]
        xl8[pl.ds(128 * n, 128), pl.ds(128 * slot, 128)] = parts[1]
        xl8[pl.ds(128 * n, 128), pl.ds(384 + 128 * slot, 128)] = parts[2]
        return parts

    for n in range(first, last):
        h, r = BLOCKS[n]
        re, im = parted(land[pl.ds(4 + n, D, stride=ROWS), :])
        block = jnp.concatenate([re.astype(F32), im.astype(F32)], axis=0).T * ends[16:17, :]
        parts = put(n, 1, block)
        if r > 0:
            put_parts(n - 1, 2, parts)
        if r < h - 1:
            put_parts(n + 1, 0, parts)
        if r == h - 1:
            side[7:8, :] = ends[h - 1 : h, :]
            side[8:72, :] = block[64:]
            put(n - h + 1, 0, jnp.concatenate([side[7:71, :], block[:64]], axis=0))
        if r == 0:
            side[80:144, :] = block[:64]
            side[144:145, :] = ends[h + 7 : h + 8, :]
            put(n + h - 1, 2, jnp.concatenate([block[64:], side[81:145, :]], axis=0))


def make_masks(jit, ex, jp, js, msk):
    for g in range(64):
        js[8 * g : 8 * g + 8, :] = jit[:, 128 * g : 128 * g + 128].astype(F32)
    for h in range(1, HARM + 1):
        even = js[pl.ds(h - 1, 64, stride=8), :]
        lhs = jnp.concatenate([even, pltpu.roll(even, 64, 1)], axis=0).astype(BF16)
        for n in range(FIRST[h], FIRST[h] + h):
            msk[pl.ds(128 * n, 128), :] = jnp.where(dot(lhs, ex[n]) == jp[n : n + 1, :], 1.0, 0.0)


def correlate(first, last, xl, xl8, taps, taps8, msk, pm):
    groups = range(first // 4, last // 4)
    pairs = max(1, 8 // len(groups))

    def one(tp):
        for g in groups:
            rows = pl.ds(512 * g, 512)
            acc = dot(xl[rows, :], taps[tp]) + dot(xl8[rows, :], taps8[tp])
            re, im = acc[:, :128], acc[:, 128:]
            kept = jnp.where(msk[rows, :] > 0.5, re * re + im * im, 0.0).astype(BF16)
            for q in range(4):
                pm[4 * g + q, pl.ds(pl.multiple_of(128 * tp, 128), 128), :] = kept[128 * q : 128 * q + 128]

    def several(step, carry):
        for k in range(pairs):
            one(pairs * step + k)
        return carry

    lax.fori_loop(0, TMPL // 2 // pairs, several, 0)


def add_harmonics(pm, e, levels, out):
    factor = jnp.exp2(2.0 * (levels[0:1, :] + levels[8:9, :] - 25.0)) * (1.0 / HARM)
    lane = lax.broadcasted_iota(jnp.int32, (64, 128), 1)
    for tp in range(TMPL // 4):
        rows = pl.ds(256 * tp, 256)
        total = jnp.zeros((256, 128), F32)
        for n in range(0, NB, 2):
            total += dot(
                jnp.concatenate([pm[n, rows, :], pm[n + 1, rows, :]], axis=1),
                jnp.concatenate([e[n], e[n + 1]], axis=0),
            )
        total = total * factor
        for q in range(2):
            even = total[128 * q : 128 * q + 64]
            odd = total[128 * q + 64 : 128 * q + 128]
            t = 4 * tp + 2 * q
            row = t // 8 * 512 + t % 8
            out[pl.ds(row, 64, stride=8), :] = jnp.where(lane < 64, even, pltpu.roll(odd, 64, 1))
            out[pl.ds(row + 1, 64, stride=8), :] = jnp.where(lane < 64, pltpu.roll(even, 64, 1), odd)


def search_kernel(*refs):
    series, coef, offset, jit, jp, w1_all = refs[:6]
    count = len(CONSTANTS)
    held = refs[6 : 6 + count]
    out = refs[6 + count]
    rest = refs[7 + count :]
    local, rest = rest[:count], rest[count:]
    xs, w1, send1, land1, send2, land2, yacc, zn, levels, send3, land3, ends, side = rest[:13]
    xl, xl8, pm, js, msk, vx, taps, taps8, const_sem, sems = rest[13:]
    me, dm = lax.axis_index("bin"), lax.axis_index("dm")
    own = [
        pltpu.make_async_copy(series, xs, const_sem.at[count]),
        pltpu.make_async_copy(w1_all.at[me], w1, const_sem.at[count + 1]),
    ]
    copies = {
        name: pltpu.make_async_copy(held[n], local[n], const_sem.at[n])
        for n, name in enumerate(CONSTANTS)
    }
    ref = dict(zip(CONSTANTS, local))
    for copy in own:
        copy.start()

    barrier = pltpu.get_barrier_semaphore()

    def greet(to):
        pl.semaphore_signal(barrier, inc=1, device_id=(dm, to), device_id_type=pl.DeviceIdType.MESH)

    for_partners(me, greet)
    for copy in copies.values():
        copy.start()
    for copy in own:
        copy.wait()
    code_samples(xs, send1)
    pl.semaphore_wait(barrier, D - 1)

    exchange(me, dm, send1, land1, 0, 8, 8, (sems.at[0], sems.at[1]))
    copies["tw1"].wait()
    wait_for(land1, 8, sems.at[1])

    def send(j, plane):
        for y in FAR:
            for z in FAR:
                if FAR[j] or y or z:
                    within = (me // 4 + y) % 4 * 4 + (me + z) % 4
                    pltpu.make_async_remote_copy(
                        src_ref=send2.at[pl.ds(pl.multiple_of(256 * j + 16 * within, 16), 16)],
                        dst_ref=land2.at[pl.ds(pl.multiple_of(16 * me, 16), 16)],
                        send_sem=sems.at[2],
                        recv_sem=sems.at[3 + j],
                        device_id=(dm, 16 * plane + within),
                        device_id_type=pl.DeviceIdType.MESH,
                    ).start()
                else:
                    land2[pl.ds(pl.multiple_of(16 * me, 16), 16), :] = send2[
                        pl.ds(pl.multiple_of(256 * j + 16 * (me % 16), 16), 16), :
                    ]

    columns(land1, w1, ref["tw1"], send2, me, send)
    make_tap_rows(coef, offset, vx, levels)
    make_taps(vx, taps, taps8)
    copies["ex"].wait()
    make_masks(jit, ref["ex"], jp, js, msk)
    for name in ("wah", "wal", "tw2", "vbh", "vbl", "e"):
        copies[name].wait()
    for h in range(1, HARM + 1):
        copies["p%d" % h].wait()

    def arrived(j):
        part = land2.at[pl.ds(0, 16 * (16 if FAR[j] else 15))]
        pltpu.make_async_copy(part, part, sems.at[3 + j]).wait()

    local_fft(
        me, arrived, land2, ref["wah"], ref["wal"], ref["tw2"], ref["vbh"], ref["vbl"], yacc, zn, levels
    )
    pack_ends(zn, levels, send3)

    def give(n):
        row, rows, first, last = CHUNKS[n]
        for h in ORDER:
            if first <= FIRST[h] < last:
                pack_harmonic(h, zn, ref["p%d" % h], send3)
        exchange(me, dm, send3, land3, row, rows, ROWS, (sems.at[7 + 2 * n], sems.at[8 + 2 * n]))

    def take(n):
        _, rows, first, last = CHUNKS[n]
        wait_for(land3, rows, sems.at[8 + 2 * n])
        if n == 0:
            unpack_ends(land3, ends, levels)
        unpack(land3, ends, first, last, side, xl, xl8)
        correlate(first, last, xl, xl8, taps, taps8, msk, pm)

    for act, n in SCHEDULE:
        (give if act else take)(n)
    add_harmonics(pm, ref["e"], levels, out)
    wait_for(land1, 8, sems.at[0])
    wait_for(land2, 16, sems.at[2])
    for n, (_, rows, _, _) in enumerate(CHUNKS):
        wait_for(land3, rows, sems.at[7 + 2 * n])


SCHEDULE = ((1, 0), (1, 1), (1, 2), (0, 0), (1, 3), (0, 1), (0, 2), (0, 3))
CONSTANTS = ("ex", "tw1", "wah", "wal", "tw2", "vbh", "vbl") + tuple(
    "p%d" % h for h in range(1, HARM + 1)
) + ("e",)


def constants():
    w1, tw1, wah, wal, tw2, vbh, vbl = fft_tables()
    e, ex, jp = select_tables()
    return [ex, tw1, wah, wal, tw2, vbh, vbl, *perm_tables(), e], jp, w1


def search(series, coef, offset, jit):
    held, jp, w1 = constants()
    whole = pl.BlockSpec(memory_space=pltpu.VMEM)
    far = pl.BlockSpec(memory_space=pl.ANY)
    return pl.pallas_call(
        search_kernel,
        out_shape=pltpu.VMEM((TMPL * 64, 128), F32),
        in_specs=[far] + [whole] * 4 + [far] * (1 + len(held)),
        out_specs=whole,
        scratch_shapes=[pltpu.VMEM(c.shape, c.dtype) for c in held]
        + [
            pltpu.VMEM((1024, 128), F32),
            pltpu.VMEM((128, D), F32),
            pltpu.VMEM((512, 128), jnp.int32),
            pltpu.VMEM((512, 128), jnp.int32),
            pltpu.VMEM((1024, 128), jnp.int32),
            pltpu.VMEM((1024, 128), jnp.int32),
            pltpu.VMEM((2 * ALPHA, 256), F32),
            pltpu.VMEM((2, 528, 128), F32),
            pltpu.VMEM((24, 128), F32),
            pltpu.VMEM((D * ROWS, 128), jnp.int32),
            pltpu.VMEM((D * ROWS, 128), jnp.int32),
            pltpu.VMEM((24, 128), F32),
            pltpu.VMEM((152, 128), F32),
            pltpu.VMEM((NB * 128, 384), BF16),
            pltpu.VMEM((NB * 128, 768), F8),
            pltpu.VMEM((NB, 1024, 128), BF16),
            pltpu.VMEM((512, 128), F32),
            pltpu.VMEM((NB * 128, 128), F32),
            pltpu.VMEM((TMPL, 8, 128), F32),
            pltpu.VMEM((TMPL // 2, 384, 256), BF16),
            pltpu.VMEM((TMPL // 2, 768, 256), F8),
            pltpu.SemaphoreType.DMA((len(held) + 2,)),
            pltpu.SemaphoreType.DMA((7 + 2 * len(CHUNKS),)),
        ],
        compiler_params=pltpu.CompilerParams(
            collective_id=0, has_side_effects=True, vmem_limit_bytes=62 * 1024 * 1024
        ),
        cost_estimate=pl.CostEstimate(flops=3 * 10**10, bytes_accessed=3 * 10**7, transcendentals=0),
    )(series, coef, offset, jit, jp, w1, *held)


def shards(series, tap_coef, tap_offset, harm_index):
    out = search(series.reshape(1024, 128), tap_coef.reshape(32, 128), tap_offset, harm_index)
    return out.reshape(2, 64, 8, 128).transpose(0, 2, 1, 3).reshape(TMPL, 8192)


def solution(mesh):
    return jax.shard_map(
        shards,
        mesh=mesh,
        in_specs=(P(("dm", "bin")), P(), P(), P(None, "bin")),
        out_specs=P(None, ("dm", "bin")),
        check_vma=False,
    )
```

profile of v0, /device:TPU:0, one launch (start us, length us, event | category | flops | bytes accessed | tf_op | source)
XLA Modules:
  0.0 62.8 jit_solution(674983011575420286)
XLA Ops:
  0.0 62.0 %shard_map.208 = f32[1024,128]{1,0:T(8,128)S(1)} custom-call(f32[1024,128]{1,0:T(8,128)} %bitcast.8, f32[32,128]{1,0:T(8,128)} %bitcast.9, s32[16,128]{1,0:T(8,128)} %refs_2_.1, s32[8,8192]{1,0:T(8,128)} %refs_3_.1, f32[36,128]{1,0:T(8,128)} %constant.36.clone.refs_4_, f32[64,128,64]{2,1,0:T(8,128)} %constant.37.clone.refs_5_, ...), custom_call_target="tpu_custom_call" | custom-call | flops 30000001024 | bytes 30000000 | tf_op jit(solution)/shard_map/pallas_call | solution.py:523
  62.0 0.8 %copy.24 = f32[16,8192]{1,0:T(8,128)} copy(f32[16,8192]{1,0:T(8,128)S(1)} %bitcast.7) | data formatting | bytes 1048576
where the time goes:
time: 62.9 us; the launch traced here: 62.8 us
  Pallas kernels  62 us (99%)
  local copies, waits for them, and re-layouts  0.8 us (1%)
    pallas_call x1, Pallas kernels, search(): pl.pallas_call(search_kernel, out_shape=pltpu.VMEM((TMPL * 64, 128), F32)...  62 us

commit v1 on v0

--- a/solution.py
+++ b/solution.py
@@ -168,13 +168,13 @@
 def make_taps(vx, taps, taps8):
     lane = lax.broadcasted_iota(jnp.int32, (64, 128), 1)
 
-    def pair(tp, carry):
+    def pair(tq, u):
         for x in range(3):
             both = []
             for z in range(2):
                 rolled = []
                 for t in range(2):
-                    row = vx[2 * tp + t, 3 * z + x : 3 * z + x + 1, :]
+                    row = vx[4 * tq + 2 * u + t, 3 * z + x : 3 * z + x + 1, :]
                     rolled.append(
                         pltpu.roll(jnp.broadcast_to(row, (64, 128)), 64 * t, 1, stride=1, stride_axis=0)
                     )
@@ -183,18 +183,23 @@
                 both.append((high, (v - high) * LOW))
 
             def put(ref, row, kind, tr, ti):
-                ref[tp, row : row + 64, 0:128] = tr.astype(kind)
-                ref[tp, row : row + 64, 128:256] = ti.astype(kind)
-                ref[tp, row + 64 : row + 128, 0:128] = (-ti).astype(kind)
-                ref[tp, row + 64 : row + 128, 128:256] = tr.astype(kind)
+                real, imag = slice(256 * u, 256 * u + 128), slice(256 * u + 128, 256 * u + 256)
+                ref[tq, row : row + 64, real] = tr.astype(kind)
+                ref[tq, row : row + 64, imag] = ti.astype(kind)
+                ref[tq, row + 64 : row + 128, real] = (-ti).astype(kind)
+                ref[tq, row + 64 : row + 128, imag] = tr.astype(kind)
 
             (rh, rl), (ih, il) = both
             put(taps, 128 * x, BF16, rh * LOW, ih * LOW)
             put(taps8, 128 * x, F8, rl, il)
             put(taps8, 384 + 128 * x, F8, rh, ih)
+
+    def four(tq, carry):
+        for u in range(2):
+            pair(tq, u)
         return carry
 
-    lax.fori_loop(0, TMPL // 2, pair, 0)
+    lax.fori_loop(0, TMPL // 4, four, 0)
 
 
 def level_of(x):
@@ -364,23 +369,25 @@
 
 def correlate(first, last, xl, xl8, taps, taps8, msk, pm):
     groups = range(first // 4, last // 4)
-    pairs = max(1, 8 // len(groups))
-
-    def one(tp):
+    fours = max(1, 4 // len(groups))
+
+    def one(tq):
         for g in groups:
             rows = pl.ds(512 * g, 512)
-            acc = dot(xl[rows, :], taps[tp]) + dot(xl8[rows, :], taps8[tp])
-            re, im = acc[:, :128], acc[:, 128:]
-            kept = jnp.where(msk[rows, :] > 0.5, re * re + im * im, 0.0).astype(BF16)
-            for q in range(4):
-                pm[4 * g + q, pl.ds(pl.multiple_of(128 * tp, 128), 128), :] = kept[128 * q : 128 * q + 128]
+            acc = dot(xl[rows, :], taps[tq]) + dot(xl8[rows, :], taps8[tq])
+            for u in range(2):
+                re, im = acc[:, 256 * u : 256 * u + 128], acc[:, 256 * u + 128 : 256 * u + 256]
+                kept = jnp.where(msk[rows, :] > 0.5, re * re + im * im, 0.0).astype(BF16)
+                to = pl.ds(pl.multiple_of(256 * tq + 128 * u, 128), 128)
+                for q in range(4):
+                    pm[4 * g + q, to, :] = kept[128 * q : 128 * q + 128]
 
     def several(step, carry):
-        for k in range(pairs):
-            one(pairs * step + k)
+        for k in range(fours):
+            one(fours * step + k)
         return carry
 
-    lax.fori_loop(0, TMPL // 2 // pairs, several, 0)
+    lax.fori_loop(0, TMPL // 4 // fours, several, 0)
 
 
 def add_harmonics(pm, e, levels, out):
@@ -546,8 +553,8 @@
             pltpu.VMEM((512, 128), F32),
             pltpu.VMEM((NB * 128, 128), F32),
             pltpu.VMEM((TMPL, 8, 128), F32),
-            pltpu.VMEM((TMPL // 2, 384, 256), BF16),
-            pltpu.VMEM((TMPL // 2, 768, 256), F8),
+            pltpu.VMEM((TMPL // 4, 384, 512), BF16),
+            pltpu.VMEM((TMPL // 4, 768, 512), F8),
             pltpu.SemaphoreType.DMA((len(held) + 2,)),
             pltpu.SemaphoreType.DMA((7 + 2 * len(CHUNKS),)),
         ],

time: 62.9 us -> 64 us (1.017)
  Pallas kernels: 62 us -> 63.1 us
    pallas_call x1, Pallas kernels: 62 us -> 63.1 us  [search(): pl.pallas_call(search_kernel, out_shape=pltpu.VMEM((TMPL * 64, 128), F32)...]
where the time goes in v1:
time: 64 us; the launch traced here: 63.9 us
  Pallas kernels  63.1 us (99%)
  local copies, waits for them, and re-layouts  0.8 us (1%)
    pallas_call x1, Pallas kernels, search(): pl.pallas_call(search_kernel, out_shape=pltpu.VMEM((TMPL * 64, 128), F32)...  63.1 us

profile of v1, /device:TPU:0, one launch (start us, length us, event | category | flops | bytes accessed | tf_op | source)
XLA Modules:
  0.0 63.9 jit_solution(16304849205805823932)
XLA Ops:
  0.0 63.1 %shard_map.208 = f32[1024,128]{1,0:T(8,128)S(1)} custom-call(f32[1024,128]{1,0:T(8,128)} %bitcast.8, f32[32,128]{1,0:T(8,128)} %bitcast.9, s32[16,128]{1,0:T(8,128)} %refs_2_.1, s32[8,8192]{1,0:T(8,128)} %refs_3_.1, f32[36,128]{1,0:T(8,128)} %constant.36.clone.refs_4_, f32[64,128,64]{2,1,0:T(8,128)} %constant.37.clone.refs_5_, ...), custom_call_target="tpu_custom_call" | custom-call | flops 30000001024 | bytes 30000000 | tf_op jit(solution)/shard_map/pallas_call | solution.py:530
  63.1 0.8 %copy.24 = f32[16,8192]{1,0:T(8,128)} copy(f32[16,8192]{1,0:T(8,128)S(1)} %bitcast.7) | data formatting | bytes 1048576

commit v2 on v0

--- a/solution.py
+++ b/solution.py
@@ -106,7 +106,9 @@
 
 
 def encode(x, bound):
-    size = jnp.sqrt(jnp.sqrt(jnp.abs(x) * (1.0 / bound)))
+    size = jnp.abs(x) * (1.0 / bound)
+    for _ in range(2):
+        size = size * lax.rsqrt(jnp.maximum(size, 1e-37))
     code = jnp.minimum(size * FULL + 0.5, FULL).astype(jnp.int32)
     return jnp.where(x < 0, -code, code)
 
@@ -405,11 +407,11 @@
 
 
 def search_kernel(*refs):
-    series, coef, offset, jit, jp, w1_all = refs[:6]
+    series, w1_all = refs[:2]
     count = len(CONSTANTS)
-    held = refs[6 : 6 + count]
-    out = refs[6 + count]
-    rest = refs[7 + count :]
+    held = refs[2 : 2 + count]
+    out = refs[2 + count]
+    rest = refs[3 + count :]
     local, rest = rest[:count], rest[count:]
     xs, w1, send1, land1, send2, land2, yacc, zn, levels, send3, land3, ends, side = rest[:13]
     xl, xl8, pm, js, msk, vx, taps, taps8, const_sem, sems = rest[13:]
@@ -432,14 +434,14 @@
         pl.semaphore_signal(barrier, inc=1, device_id=(dm, to), device_id_type=pl.DeviceIdType.MESH)
 
     for_partners(me, greet)
-    for copy in copies.values():
-        copy.start()
     for copy in own:
         copy.wait()
     code_samples(xs, send1)
     pl.semaphore_wait(barrier, D - 1)
 
     exchange(me, dm, send1, land1, 0, 8, 8, (sems.at[0], sems.at[1]))
+    for copy in copies.values():
+        copy.start()
     copies["tw1"].wait()
     wait_for(land1, 8, sems.at[1])
 
@@ -462,10 +464,11 @@
                     ]
 
     columns(land1, w1, ref["tw1"], send2, me, send)
-    make_tap_rows(coef, offset, vx, levels)
+    for name in ("coef", "offset", "jit", "jp", "ex"):
+        copies[name].wait()
+    make_tap_rows(ref["coef"], ref["offset"], vx, levels)
     make_taps(vx, taps, taps8)
-    copies["ex"].wait()
-    make_masks(jit, ref["ex"], jp, js, msk)
+    make_masks(ref["jit"], ref["ex"], ref["jp"], js, msk)
     for name in ("wah", "wal", "tw2", "vbh", "vbl", "e"):
         copies[name].wait()
     for h in range(1, HARM + 1):
@@ -505,7 +508,7 @@
 
 
 SCHEDULE = ((1, 0), (1, 1), (1, 2), (0, 0), (1, 3), (0, 1), (0, 2), (0, 3))
-CONSTANTS = ("ex", "tw1", "wah", "wal", "tw2", "vbh", "vbl") + tuple(
+CONSTANTS = ("tw1", "coef", "offset", "jit", "jp", "ex", "wah", "wal", "tw2", "vbh", "vbl") + tuple(
     "p%d" % h for h in range(1, HARM + 1)
 ) + ("e",)
 
@@ -513,17 +516,18 @@
 def constants():
     w1, tw1, wah, wal, tw2, vbh, vbl = fft_tables()
     e, ex, jp = select_tables()
-    return [ex, tw1, wah, wal, tw2, vbh, vbl, *perm_tables(), e], jp, w1
+    return [tw1], [jp, ex, wah, wal, tw2, vbh, vbl, *perm_tables(), e], w1
 
 
 def search(series, coef, offset, jit):
-    held, jp, w1 = constants()
+    first, later, w1 = constants()
+    held = first + [coef, offset, jit] + later
     whole = pl.BlockSpec(memory_space=pltpu.VMEM)
     far = pl.BlockSpec(memory_space=pl.ANY)
     return pl.pallas_call(
         search_kernel,
         out_shape=pltpu.VMEM((TMPL * 64, 128), F32),
-        in_specs=[far] + [whole] * 4 + [far] * (1 + len(held)),
+        in_specs=[far] * (2 + len(held)),
         out_specs=whole,
         scratch_shapes=[pltpu.VMEM(c.shape, c.dtype) for c in held]
         + [
@@ -555,7 +559,7 @@
             collective_id=0, has_side_effects=True, vmem_limit_bytes=62 * 1024 * 1024
         ),
         cost_estimate=pl.CostEstimate(flops=3 * 10**10, bytes_accessed=3 * 10**7, transcendentals=0),
-    )(series, coef, offset, jit, jp, w1, *held)
+    )(series, w1, *held)
 
 
 def shards(series, tap_coef, tap_offset, harm_index):

time: 62.9 us -> 61.6 us (0.979)
  Pallas kernels: 62 us -> 60.7 us
    pallas_call x1, Pallas kernels: 62 us -> 60.7 us  [search(): pl.pallas_call(search_kernel, out_shape=pltpu.VMEM((TMPL * 64, 128), F32)...]
where the time goes in v2:
time: 61.6 us; the launch traced here: 61.5 us
  Pallas kernels  60.7 us (99%)
  local copies, waits for them, and re-layouts  0.8 us (1%)
    pallas_call x1, Pallas kernels, search(): pl.pallas_call(search_kernel, out_shape=pltpu.VMEM((TMPL * 64, 128), F32)...  60.7 us

profile of v2, /device:TPU:0, one launch (start us, length us, event | category | flops | bytes accessed | tf_op | source)
XLA Modules:
  0.0 61.5 jit_solution(4102680198050298507)
XLA Ops:
  0.0 60.7 %shard_map.208 = f32[1024,128]{1,0:T(8,128)S(1)} custom-call(f32[1024,128]{1,0:T(8,128)} %bitcast.8, f32[64,128,64]{2,1,0:T(8,128)} %constant.36.clone.refs_1_, f32[2,64,2048]{2,1,0:T(8,128)} %constant.37.clone.refs_2_, f32[32,128]{1,0:T(8,128)} %bitcast.9, s32[16,128]{1,0:T(8,128)} %refs_4_.1, s32[8,8192]{1,0:T(8,128)} %refs_5_.1, ...), custom_call_target="tpu_custom_call" | custom-call | flops 30000001024 | bytes 30000000 | tf_op jit(solution)/shard_map/pallas_call | solution.py:527
  60.7 0.8 %copy.24 = f32[16,8192]{1,0:T(8,128)} copy(f32[16,8192]{1,0:T(8,128)S(1)} %bitcast.7) | data formatting | bytes 1048576

commit v3 on v2

--- a/solution.py
+++ b/solution.py
@@ -62,7 +62,7 @@
     w1 = w1.reshape(D, 2, 4, 16, D)
     w1 = np.stack([w1[e][:, [(e // 16 + f) % 4 for f in FAR]] for e in range(D)]).reshape(D, 2 * D, D)
     wa = wa.reshape(2 * ALPHA, 2, 4, 128).transpose(2, 0, 1, 3).reshape(4, 2 * ALPHA, 256)
-    return w1.astype(np.float32), tw1, *np_split(wa), tw2, *np_split(vb)
+    return w1.astype(np.float32), tw1, *np_split(wa), tw2, *np_split(vb.T)
 
 
 @functools.lru_cache(None)
@@ -99,6 +99,10 @@
 
 def dot(a, b):
     return jnp.dot(a, b, preferred_element_type=F32)
+
+
+def dot_rows(a, b):
+    return lax.dot_general(a, b, (((1,), (1,)), ((), ())), preferred_element_type=F32)
 
 
 def dot3(ah, al, bh, bl):
@@ -262,13 +266,13 @@
     yr, yi = y[:ALPHA], y[ALPHA:]
     t = jnp.concatenate([yr * tw[0] - yi * tw[1], yr * tw[1] + yi * tw[0]], axis=1)
     th, tl = split(t)
-    z = dot3(th, tl, vbh[...], vbl[...])
+    z = dot_rows(vbh[...], th) + dot_rows(vbl[...], th) + dot_rows(vbh[...], tl)
     level = level_of(z)
     levels[16:24, :] = jnp.broadcast_to(level, (8, 128))
     z = jnp.clip(jnp.round(z * (jnp.exp2(-level) * FULL)), -FULL, FULL)
     zero = jnp.zeros((8, 128), F32)
     for c in range(2):
-        zt = z[:, 128 * c : 128 * c + 128].T
+        zt = z[128 * c : 128 * c + 128]
         zn[c, 0:8, :] = zero
         zn[c, 520:528, :] = zero
         for n in range(4):

time: 61.6 us -> 61.6 us (level)
  no operation moved by 1% of the time
where the time goes in v3:
time: 61.6 us; the launch traced here: 61.5 us
  Pallas kernels  60.7 us (99%)
  local copies, waits for them, and re-layouts  0.8 us (1%)
    pallas_call x1, Pallas kernels, search(): pl.pallas_call(search_kernel, out_shape=pltpu.VMEM((TMPL * 64, 128), F32)...  60.7 us

profile of v3, /device:TPU:0, one launch (start us, length us, event | category | flops | bytes accessed | tf_op | source)
XLA Modules:
  0.0 61.5 jit_solution(97360687531930118)
XLA Ops:
  0.0 60.7 %shard_map.208 = f32[1024,128]{1,0:T(8,128)S(1)} custom-call(f32[1024,128]{1,0:T(8,128)} %bitcast.8, f32[64,128,64]{2,1,0:T(8,128)} %constant.36.clone.refs_1_, f32[2,64,2048]{2,1,0:T(8,128)} %constant.37.clone.refs_2_, f32[32,128]{1,0:T(8,128)} %bitcast.9, s32[16,128]{1,0:T(8,128)} %refs_4_.1, s32[8,8192]{1,0:T(8,128)} %refs_5_.1, ...), custom_call_target="tpu_custom_call" | custom-call | flops 30000001024 | bytes 30000000 | tf_op jit(solution)/shard_map/pallas_call | solution.py:531
  60.7 0.8 %copy.24 = f32[16,8192]{1,0:T(8,128)} copy(f32[16,8192]{1,0:T(8,128)S(1)} %bitcast.7) | data formatting | bytes 1048576
